TPU v7x, 128 devices: a whole 4x4x4 slice. The times are simulated.
128 devices in a mesh: lag: 8 (over z_hi, y), patch: 16 (over z_lo, x, core).
Axes of the slice: x: 4, y: 4, z: 4 (z_hi: 2, z_lo: 2; z = z_hi * 2 + z_lo), core: 2. Of those that a mesh axis runs over, the one named last changes fastest.
Arguments:
- excitation: float32 [4, 16384, 128], P(None, 'patch'), may hold values from -6 to 6
- pending: float32 [24, 16384, 128], P('lag', 'patch'), may hold values from -6 to 6
- retarded_blocks: bfloat16 [24, 128, 16, 128, 128], P('lag', 'patch'), may hold values from -0.02734375 to 0.02734375
- column_index: int32 [24, 128, 16], P('lag', 'patch'), may hold values from 0 to 127, all different within a row
- near_inverse: float32 [64, 128, 128], P('patch'), may hold values from -1 to 4
- near_index: int32 [128], P('patch'), may hold values from 0 to 3
Outputs:
- currents: bfloat16 [4, 16384, 128], P(None, 'patch')
- final_sums: float32 [24, 16384, 128], P('lag', 'patch')
Inputs may be any that keep to these rules, and one draw needn't show every extreme that they name: `column_index`: each block row of each lag names 16 different column blocks. `near_index`: an index into the 4 inverses of the block row's own slab.
All inputs are finite; a program needn't handle non-finite values.
Results may differ from a plain program's by a relative error of at most 0.0034.
Values may be sent and summed in bfloat16 or wider, within the bound.
A program may use at most 128 MiB of HBM per device.

v0:
```python
import jax
import jax.numpy as jnp
from jax import lax
from jax.sharding import PartitionSpec as P


def from_root(block, axis, holder):
    block = jnp.where(lax.axis_index(axis) == holder, block, jnp.zeros_like(block))
    return lax.psum(block, axis)


def from_behind(x, axis, by):
    size = lax.axis_size(axis)
    pairs = [(i, i + by) for i in range(size) if 0 <= i + by < size]
    return lax.ppermute(x, axis, pairs)


def solve_rows(rhs, inverses, block_size):
    width = rhs.shape[1]
    blocks = rhs.reshape(-1, block_size, width)
    solved = jnp.einsum(
        "bij,bje->bie",
        inverses,
        blocks,
        precision=lax.Precision.HIGHEST,
        preferred_element_type=jnp.float32,
    )
    return solved.reshape(-1, width).astype(jnp.bfloat16)


def per_device(excitation, pending, retarded_blocks, column_index, near_inverse, near_index):
    block_size = retarded_blocks.shape[3]
    width = excitation.shape[2]
    lag_count = pending.shape[0]
    slab_rows = excitation.shape[1]
    inverses = near_inverse[near_index]
    waiting = pending
    currents = []
    for moment in range(excitation.shape[0]):
        lowest = waiting[0]
        retarded = from_root(lowest, "lag", 0)
        current = solve_rows(excitation[moment] - retarded, inverses, block_size)
        incoming = from_behind(lowest, "lag", -1)
        gathered = lax.all_gather(current, "patch", axis=0, tiled=True)
        currents.append(current)
        blocks = gathered.reshape(-1, block_size, width)
        picked = blocks[column_index]
        lag_terms = jnp.einsum(
            "lbkij,lbkje->lbie", retarded_blocks, picked, preferred_element_type=jnp.float32
        )
        lag_terms = lag_terms.reshape(lag_count, slab_rows, width)
        shifted = jnp.concatenate([waiting[1:], incoming[None]], axis=0)
        waiting = lag_terms + shifted
    return (jnp.stack(currents), waiting)


def solution(mesh):
    placed = (
        P(None, "patch", None),
        P("lag", "patch", None),
        P("lag", "patch", None, None, None),
        P("lag", "patch", None),
        P("patch", None, None),
        P("patch"),
    )
    return jax.shard_map(
        per_device,
        mesh=mesh,
        in_specs=placed,
        out_specs=(P(None, "patch", None), P("lag", "patch", None)),
        check_vma=False,
    )
```

profile of v0, /device:TPU:25, one launch (start us, length us, event | category | flops | bytes accessed | tf_op | source)
XLA Modules:
  0.0 625.2 jit_solution(13839233985507256124)
XLA Ops:
  7.2 2.0 broadcast_select_fusion.3
  10.6 81.1 %all-reduce.5.cloned.1.call-done = f32[1024,128]{1,0:T(8,128)} async-done(((f32[1024,128]{1,0:T(8,128)}), f32[1024,128]{1,0:T(8,128)}) %all-reduce.5.cloned.1.call-update) | async-done | bytes 524304 | tf_op jit(solution)/shard_map/psum | solution.py:9
  91.7 1.3 bitcast_subtract_fusion.3
  92.9 1.3 convolution_convert_fusion.3
  94.4 1.9 collective-permute-start
  96.4 40.7 %all-gather.5.cloned.1.call-done = bf16[16384,128]{1,0:T(8,128)(2,1)} async-done(((bf16[1024,128]{1,0:T(8,128)(2,1)}), bf16[16384,128]{1,0:T(8,128)(2,1)}) %all-gather.5.cloned.1.call-update) | async-done | bytes 4194320 | tf_op jit(solution)/shard_map/all_gather | solution.py:44
  137.2 13.5 %gather_fusion.1 = bf16[384,128,128]{2,1,0:T(8,128)(2,1)} fusion(bf16[128,128,128]{2,1,0:T(8,128)(2,1)} %bitcast.96, s32[1024]{0:T(1024)S(1)} %pad_clamp_fusion), kind=kCustom, calls=%fused_computation.1 | custom fusion | bytes 25167360 | tf_op jit(solution)/shard_map/gather | solution.py:47
  150.6 11.7 %fusion = f32[3,8,128,128,1]{2,3,4,1,0:T(8,128)S(1)} fusion(bf16[3,8,16,128,128]{4,3,2,1,0:T(8,128)(2,1)} %param.8, bf16[3,8,16,128,128]{4,3,2,1,0:T(8,128)(2,1)} %bitcast.93), kind=kOutput, calls=%fused_computation.30 | convolution fusion | flops 1610612736 | bytes 26738688 | tf_op jit(solution)/shard_map/lbkij,lbkje->lbie/dot_general | solution.py:48
  162.6 0.9 broadcast_select_fusion.2
  163.6 79.7 %all-reduce.7.cloned.1.call-done = f32[1024,128]{1,0:T(8,128)} async-done(((f32[1024,128]{1,0:T(8,128)}), f32[1024,128]{1,0:T(8,128)}) %all-reduce.7.cloned.1.call-update) | async-done | bytes 524304 | tf_op jit(solution)/shard_map/psum | solution.py:9
  243.2 1.3 bitcast_subtract_fusion.2
  244.5 1.3 convolution_convert_fusion.2
  245.9 2.1 collective-permute-start.1
  248.0 40.7 %all-gather.7.cloned.1.call-done = bf16[16384,128]{1,0:T(8,128)(2,1)} async-done(((bf16[1024,128]{1,0:T(8,128)(2,1)}), bf16[16384,128]{1,0:T(8,128)(2,1)}) %all-gather.7.cloned.1.call-update) | async-done | bytes 4194320 | tf_op jit(solution)/shard_map/all_gather | solution.py:44
  288.7 13.5 %gather_fusion.2 = bf16[384,128,128]{2,1,0:T(8,128)(2,1)} fusion(bf16[128,128,128]{2,1,0:T(8,128)(2,1)} %bitcast.98, s32[1024]{0:T(1024)S(1)} %pad_clamp_fusion), kind=kCustom, calls=%fused_computation.2 | custom fusion | bytes 25167360 | tf_op jit(solution)/shard_map/gather | solution.py:47
  302.2 11.7 %fusion.1 = f32[3,8,128,128,1]{2,3,4,1,0:T(8,128)S(1)} fusion(bf16[3,8,16,128,128]{4,3,2,1,0:T(8,128)(2,1)} %param.8, bf16[3,8,16,128,128]{4,3,2,1,0:T(8,128)(2,1)} %bitcast.94), kind=kOutput, calls=%fused_computation.31 | convolution fusion | flops 1610612736 | bytes 26738688 | tf_op jit(solution)/shard_map/lbkij,lbkje->lbie/dot_general | solution.py:48
  315.1 79.7 %all-reduce.9.cloned.1.call-done = f32[1024,128]{1,0:T(8,128)} async-done(((f32[1024,128]{1,0:T(8,128)}), f32[1024,128]{1,0:T(8,128)}) %all-reduce.9.cloned.1.call-update) | async-done | bytes 524304 | tf_op jit(solution)/shard_map/psum | solution.py:9
  394.8 1.3 bitcast_subtract_fusion.1
  396.0 1.4 convolution_convert_fusion.1
  397.5 2.1 collective-permute-start.2
  399.6 40.6 %all-gather.9.cloned.1.call-done = bf16[16384,128]{1,0:T(8,128)(2,1)} async-done(((bf16[1024,128]{1,0:T(8,128)(2,1)}), bf16[16384,128]{1,0:T(8,128)(2,1)}) %all-gather.9.cloned.1.call-update) | async-done | bytes 4194320 | tf_op jit(solution)/shard_map/all_gather | solution.py:44
  440.3 13.5 %gather_fusion.3 = bf16[384,128,128]{2,1,0:T(8,128)(2,1)} fusion(bf16[128,128,128]{2,1,0:T(8,128)(2,1)} %bitcast.99, s32[1024]{0:T(1024)S(1)} %pad_clamp_fusion), kind=kCustom, calls=%fused_computation.3 | custom fusion | bytes 25167360 | tf_op jit(solution)/shard_map/gather | solution.py:47
  453.7 11.7 %fusion.2 = f32[3,8,128,128,1]{2,3,4,1,0:T(8,128)S(1)} fusion(bf16[3,8,16,128,128]{4,3,2,1,0:T(8,128)(2,1)} %param.8, bf16[3,8,16,128,128]{4,3,2,1,0:T(8,128)(2,1)} %bitcast.95), kind=kOutput, calls=%fused_computation.32 | convolution fusion | flops 1610612736 | bytes 26738688 | tf_op jit(solution)/shard_map/lbkij,lbkje->lbie/dot_general | solution.py:48
  466.6 79.7 %all-reduce.11.cloned.1.call-done = f32[1024,128]{1,0:T(8,128)} async-done(((f32[1024,128]{1,0:T(8,128)}), f32[1024,128]{1,0:T(8,128)}) %all-reduce.11.cloned.1.call-update) | async-done | bytes 524304 | tf_op jit(solution)/shard_map/psum | solution.py:9
  546.3 1.3 bitcast_subtract_fusion
  547.6 1.3 convolution_convert_fusion
  549.0 2.2 collective-permute-start.3
  551.2 2.1 pad_maximum_fusion
  553.3 38.5 %all-gather.11.cloned.1.call-done = bf16[16384,128]{1,0:T(8,128)(2,1)} async-done(((bf16[1024,128]{1,0:T(8,128)(2,1)}), bf16[16384,128]{1,0:T(8,128)(2,1)}) %all-gather.11.cloned.1.call-update) | async-done | bytes 4194320 | tf_op jit(solution)/shard_map/all_gather | solution.py:44
  591.8 13.5 %gather_fusion.4 = bf16[384,128,128]{2,1,0:T(8,128)(2,1)} fusion(bf16[128,128,128]{2,1,0:T(8,128)(2,1)} %bitcast.97, s32[1024]{0:T(1024)S(1)} %pad_clamp_fusion), kind=kCustom, calls=%fused_computation.4 | custom fusion | bytes 25167360 | tf_op jit(solution)/shard_map/gather | solution.py:47
  605.3 11.7 %fusion.3 = f32[3,8,128,128,1]{2,3,4,1,0:T(8,128)S(1)} fusion(bf16[3,8,16,128,128]{4,3,2,1,0:T(8,128)(2,1)} %param.8, bf16[3,8,16,128,128]{4,3,2,1,0:T(8,128)(2,1)} %bitcast.92), kind=kOutput, calls=%fused_computation.33 | convolution fusion | flops 1610612736 | bytes 26738688 | tf_op jit(solution)/shard_map/lbkij,lbkje->lbie/dot_general | solution.py:48
  617.0 1.4 maximum_add_fusion.3
  (63 shorter events, 4.4 us)
Async XLA Ops:
  7.2 2.8 copy-start
  7.2 87.2 %copy-start.5 = (f32[3,1024,128]{2,1,0:T(8,128)S(1)}, f32[3,1024,128]{2,1,0:T(8,128)}, u32[]{:S(2)}) copy-start(f32[3,1024,128]{2,1,0:T(8,128)} %param.7) | copy-start | bytes 4718596
  7.2 84.5 %all-reduce.5.cloned.1.call-start = ((), (), s32[]{:S(2)}) async-start(), calls=%async_computation | async-start | bytes 1048576 | tf_op jit(solution)/shard_map/psum | solution.py:9
  9.2 87.1 %copy-start.9 = (s32[3,8,16]{2,1,0:T(8,128)S(1)}, s32[3,8,16]{2,1,0:T(8,128)}, u32[]{:S(2)}) copy-start(s32[3,8,16]{2,1,0:T(8,128)} %param.9) | copy-start | bytes 4612
  9.3 127.9 %all-gather.5.cloned.1.call-start = ((), (), s32[]{:S(2)}) async-start(), calls=%async_computation.1 | async-start | bytes 4456448 | tf_op jit(solution)/shard_map/all_gather | solution.py:44
  94.3 148.9 %all-reduce.7.cloned.1.call-start = ((), (), s32[]{:S(2)}) async-start(), calls=%async_computation.2 | async-start | bytes 1048576 | tf_op jit(solution)/shard_map/psum | solution.py:9
  94.4 67.9 %collective-permute-start = (f32[1024,128]{1,0:T(8,128)S(1)}, f32[1024,128]{1,0:T(8,128)S(1)}, u32[]{:S(2)}, u32[]{:S(2)}) collective-permute-start(f32[1024,128]{1,0:T(8,128)S(1)} %slice_bitcast_fusion.3), channel_id=1, source_target_pairs={{16,0},{32,16},{48,32},{64,48},{80,64},{96,80},{112,96},{17,1},{33... | collective-permute-start | bytes 1572872 | tf_op jit(solution)/shard_map/ppermute | solution.py:15
  150.6 11.7 %slice-start.3 = ((f32[3,1024,128]{2,1,0:T(8,128)}), f32[2,1024,128]{2,1,0:T(8,128)S(1)}, s32[]{:S(2)}) async-start(f32[3,1024,128]{2,1,0:T(8,128)} %param.7), calls=%async_computation.11 | async-start | bytes 2097152 | tf_op jit(solution)/shard_map/slice | solution.py:52
  162.6 139.6 %copy-start.2 = (f32[3,1024,128]{2,1,0:T(8,128)}, f32[3,1024,128]{2,1,0:T(8,128)S(1)}, u32[]{:S(2)}) copy-start(f32[3,1024,128]{2,1,0:T(8,128)S(1)} %maximum_add_fusion) | copy-start | bytes 4718596
  163.5 125.2 %all-gather.7.cloned.1.call-start = ((), (), s32[]{:S(2)}) async-start(), calls=%async_computation.3 | async-start | bytes 4456448 | tf_op jit(solution)/shard_map/all_gather | solution.py:44
  245.8 148.9 %all-reduce.9.cloned.1.call-start = ((), (), s32[]{:S(2)}) async-start(), calls=%async_computation.4 | async-start | bytes 1048576 | tf_op jit(solution)/shard_map/psum | solution.py:9
  245.9 67.9 %collective-permute-start.1 = (f32[1024,128]{1,0:T(8,128)S(1)}, f32[1024,128]{1,0:T(8,128)S(1)}, u32[]{:S(2)}, u32[]{:S(2)}) collective-permute-start(f32[1024,128]{1,0:T(8,128)S(1)} %slice_bitcast_fusion.2), channel_id=1, source_target_pairs={{16,0},{32,16},{48,32},{64,48},{80,64},{96,80},{112,96},{17,1},{33... | collective-permute-start | bytes 1572872 | tf_op jit(solution)/shard_map/ppermute | solution.py:15
  302.2 11.7 %slice-start = ((f32[3,1024,128]{2,1,0:T(8,128)}), f32[2,1024,128]{2,1,0:T(8,128)S(1)}, s32[]{:S(2)}) async-start(f32[3,1024,128]{2,1,0:T(8,128)} %copy-done.2), calls=%async_computation.8 | async-start | bytes 2097152 | tf_op jit(solution)/shard_map/slice | solution.py:52
  314.1 139.6 %copy-start.3 = (f32[3,1024,128]{2,1,0:T(8,128)}, f32[3,1024,128]{2,1,0:T(8,128)S(1)}, u32[]{:S(2)}) copy-start(f32[3,1024,128]{2,1,0:T(8,128)S(1)} %maximum_add_fusion.1) | copy-start | bytes 4718596
  315.0 125.2 %all-gather.9.cloned.1.call-start = ((), (), s32[]{:S(2)}) async-start(), calls=%async_computation.5 | async-start | bytes 4456448 | tf_op jit(solution)/shard_map/all_gather | solution.py:44
  397.4 148.9 %all-reduce.11.cloned.1.call-start = ((), (), s32[]{:S(2)}) async-start(), calls=%async_computation.6 | async-start | bytes 1048576 | tf_op jit(solution)/shard_map/psum | solution.py:9
  397.5 67.9 %collective-permute-start.2 = (f32[1024,128]{1,0:T(8,128)S(1)}, f32[1024,128]{1,0:T(8,128)S(1)}, u32[]{:S(2)}, u32[]{:S(2)}) collective-permute-start(f32[1024,128]{1,0:T(8,128)S(1)} %slice_bitcast_fusion.1), channel_id=1, source_target_pairs={{16,0},{32,16},{48,32},{64,48},{80,64},{96,80},{112,96},{17,1},{33... | collective-permute-start | bytes 1572872 | tf_op jit(solution)/shard_map/ppermute | solution.py:15
  453.7 11.7 %slice-start.1 = ((f32[3,1024,128]{2,1,0:T(8,128)}), f32[2,1024,128]{2,1,0:T(8,128)S(1)}, s32[]{:S(2)}) async-start(f32[3,1024,128]{2,1,0:T(8,128)} %copy-done.3), calls=%async_computation.9 | async-start | bytes 2097152 | tf_op jit(solution)/shard_map/slice | solution.py:52
  465.7 87.6 %copy-start.4 = (f32[3,1024,128]{2,1,0:T(8,128)}, f32[3,1024,128]{2,1,0:T(8,128)S(1)}, u32[]{:S(2)}) copy-start(f32[3,1024,128]{2,1,0:T(8,128)S(1)} %maximum_add_fusion.2) | copy-start | bytes 4718596
  465.7 85.5 %copy-start.6 = (bf16[8,128,128]{2,1,0:T(8,128)(2,1)S(1)}, bf16[8,128,128]{2,1,0:T(8,128)(2,1)}, u32[]{:S(2)}) copy-start(bf16[8,128,128]{2,1,0:T(8,128)(2,1)} %convolution_convert_fusion.3) | copy-start | bytes 786436
  465.7 85.5 %copy-start.7 = (bf16[8,128,128]{2,1,0:T(8,128)(2,1)S(1)}, bf16[8,128,128]{2,1,0:T(8,128)(2,1)}, u32[]{:S(2)}) copy-start(bf16[8,128,128]{2,1,0:T(8,128)(2,1)} %convolution_convert_fusion.2) | copy-start | bytes 786436
  465.7 85.5 %copy-start.8 = (bf16[8,128,128]{2,1,0:T(8,128)(2,1)S(1)}, bf16[8,128,128]{2,1,0:T(8,128)(2,1)}, u32[]{:S(2)}) copy-start(bf16[8,128,128]{2,1,0:T(8,128)(2,1)} %convolution_convert_fusion.1) | copy-start | bytes 786436
  466.6 125.2 %all-gather.11.cloned.1.call-start = ((), (), s32[]{:S(2)}) async-start(), calls=%async_computation.7 | async-start | bytes 4456448 | tf_op jit(solution)/shard_map/all_gather | solution.py:44
  549.0 68.0 %collective-permute-start.3 = (f32[1024,128]{1,0:T(8,128)S(1)}, f32[1024,128]{1,0:T(8,128)S(1)}, u32[]{:S(2)}, u32[]{:S(2)}) collective-permute-start(f32[1024,128]{1,0:T(8,128)S(1)} %slice_bitcast_fusion), channel_id=1, source_target_pairs={{16,0},{32,16},{48,32},{64,48},{80,64},{96,80},{112,96},{17,1},{33... | collective-permute-start | bytes 1572872 | tf_op jit(solution)/shard_map/ppermute | solution.py:15
  605.3 11.7 %slice-start.2 = ((f32[3,1024,128]{2,1,0:T(8,128)}), f32[2,1024,128]{2,1,0:T(8,128)S(1)}, s32[]{:S(2)}) async-start(f32[3,1024,128]{2,1,0:T(8,128)} %copy-done.4), calls=%async_computation.10 | async-start | bytes 2097152 | tf_op jit(solution)/shard_map/slice | solution.py:52
  605.3 13.1 %copy-start.1 = (f32[4,128,128]{2,1,0:T(8,128)S(1)}, f32[4,128,128]{2,1,0:T(8,128)}, u32[]{:S(2)}) copy-start(f32[4,128,128]{2,1,0:T(8,128)} %param.10) | copy-start | bytes 786436
Sparse Core Ops, SparseCore 0:
  11.1 80.5 all-reduce.4
  94.4 42.6 all-gather.4
  163.6 79.5 all-reduce.6
  246.0 42.6 all-gather.6
  315.2 79.5 all-reduce.8
  397.5 42.6 all-gather.8
  466.7 79.5 all-reduce.10
  549.1 42.6 all-gather.10
where the time goes:
time: 627 us; the launch traced here: 625 us
  waiting for transfers between devices  481 us (77%)
  local copies, waits for them, and re-layouts  54.8 us (9%)
  matrix products  52.1 us (8%)
  other arithmetic  14.4 us (2%)
  between operations  14.4 us (2%)
  starting transfers between devices  8.67 us (1%)
    psum x4, waiting for transfers between devices, from_root(): return lax.psum(block, axis)  320 us
    all_gather x4, waiting for transfers between devices, per_device(): gathered = lax.all_gather(current, 'patch', axis=0, tiled=True)  161 us
    gather x4, local copies, waits for them, and re-layouts, per_device(): picked = blocks[column_index]  53.9 us
    dot_general x4, matrix products, per_device(): jnp.einsum('lbkij,lbkje->lbie', retarded_blocks, picked, preferred_elemen...  46.7 us
  transfers between devices with their start and end apart: 12, of which 8 were waited for; matrix products, arithmetic and copies ran while one was open for 17% of the time, Pallas kernels for 0%

commit v1 on v0

v1 whole, which is shorter than its diff:
```python
import functools

import jax
import jax.numpy as jnp
from jax import lax
from jax.experimental import pallas as pl
from jax.experimental.pallas import tpu as pltpu
from jax.sharding import PartitionSpec as P

MESH = pl.DeviceIdType.MESH
BLK = 128
WIDTH = 128
ROWS = 1024
BLOCKS = 8
A_BLOCKS = 5
SHIFTS = (1, 3, 2)

OWN, FROM_X, FROM_Z, DIAG_A, DIAG_B, SIB, BEHIND, N_RECV = 0, 1, 4, 5, 8, 11, 22, 23
LAG_SEND = 23
N_SEND = 26


def kernel(
    steps,
    column_ref, near_ref, excitation_hbm, pending_hbm, weights_hbm, inverse_hbm,
    currents_hbm, sums_hbm,
    x0, x1, x2, x3, weights, excitation, inverse, waiting, behind0, behind, ahead,
    load_sem, store_sem, send_sem, recv_sem,
):
    fields = (x0, x1, x2, x3)
    lag, patch = lax.axis_index("lag"), lax.axis_index("patch")
    z_hi, y = lag // 4, lag % 4
    z_lo, x, core = patch // 8, (patch // 2) % 4, patch % 2

    def at(x=x, z_lo=z_lo, core=core, y=y, z_hi=z_hi):
        return (z_hi * 4 + y, z_lo * 8 + x * 2 + core)

    def held(x=x, z_lo=z_lo, core=core):
        return ((z_lo + z_hi) % 2) * 8 + x * 2 + core

    other_z, other_core = 1 - z_lo, 1 - core
    x_to = [(x + s) % 4 for s in SHIFTS]
    x_from = [(x + 4 - s) % 4 for s in SHIFTS]

    loads = [
        pltpu.make_async_copy(pending_hbm, waiting, load_sem.at[0]),
        pltpu.make_async_copy(inverse_hbm, inverse, load_sem.at[1]),
        pltpu.make_async_copy(excitation_hbm, excitation, load_sem.at[2]),
        pltpu.make_async_copy(weights_hbm, weights, load_sem.at[3]),
    ]
    for copy in loads:
        copy.start()

    barrier = pltpu.get_barrier_semaphore()
    greeted = [at(x=to) for to in x_to] + [at(y=(y + s) % 4) for s in SHIFTS]
    greeted += [at(z_lo=other_z), at(core=other_core), at(z_lo=other_z, z_hi=1 - z_hi), at(y=3 - y, z_hi=1 - z_hi)]
    for device in greeted:
        pl.semaphore_signal(barrier, inc=1, device_id=device, device_id_type=MESH)
    pl.semaphore_wait(barrier, len(greeted))

    def piece(t, slab, low=0, high=BLOCKS):
        return fields[t].at[pl.ds(slab * BLOCKS + low, high - low)]

    def copy(t, ref, device, index, sender=None):
        return pltpu.make_async_remote_copy(
            src_ref=ref,
            dst_ref=ref,
            send_sem=send_sem.at[t, index if sender is None else sender],
            recv_sem=recv_sem.at[t, index],
            device_id=device,
            device_id_type=MESH,
        )

    me = at()

    def to_sibling(t, ref, index):
        copy(t, ref, at(core=other_core), SIB + index).start()

    def along_y(t):
        for i, s in enumerate(SHIFTS):
            copy(t, piece(t, held()), at(y=(y + s) % 4), OWN, LAG_SEND + i).start()

    def first_sends(t):
        own = piece(t, held())
        for i, to in enumerate(x_to):
            copy(t, own, at(x=to), FROM_X + i).start()
        copy(t, own, at(z_lo=other_z), FROM_Z).start()
        to_sibling(t, own, 0)

    def relays(t):
        def arrived(ref, index):
            copy(t, ref, me, index).wait_recv()

        def from_z():
            ref = piece(t, held(z_lo=other_z))
            arrived(ref, FROM_Z)
            for i, to in enumerate(x_to):
                copy(t, piece(t, held(z_lo=other_z), A_BLOCKS), at(x=to), DIAG_B + i).start()
            to_sibling(t, ref, 4)

        def from_x(i):
            ref = piece(t, held(x=x_from[i]))
            arrived(ref, FROM_X + i)
            copy(t, piece(t, held(x=x_from[i]), 0, A_BLOCKS), at(z_lo=other_z), DIAG_A + i).start()
            to_sibling(t, ref, 1 + i)

        from_z()
        for i in range(3):
            from_x(i)
        for i in range(3):
            slab = held(x=x_from[i], z_lo=other_z)
            for ref, index in ((piece(t, slab, 0, A_BLOCKS), 0), (piece(t, slab, A_BLOCKS), 3)):
                arrived(ref, DIAG_A + index + i)
                to_sibling(t, ref, 5 + index + i)
        arrived(piece(t, held(core=other_core)), SIB)
        arrived(piece(t, held(z_lo=other_z, core=other_core)), SIB + 4)
        for i in range(3):
            arrived(piece(t, held(x=x_from[i], core=other_core)), SIB + 1 + i)
            slab = held(x=x_from[i], z_lo=other_z, core=other_core)
            arrived(piece(t, slab, 0, A_BLOCKS), SIB + 5 + i)
            arrived(piece(t, slab, A_BLOCKS), SIB + 8 + i)

    def solve(t):
        for b in range(ROWS // BLK):
            rows = pl.ds(b * BLK, BLK)
            rhs = excitation[t, rows, :] - waiting[0, rows, :]
            solved = jnp.dot(
                inverse[near_ref[b]], rhs, precision=lax.Precision.HIGHEST, preferred_element_type=jnp.float32
            )
            fields[t][held() * BLOCKS + b] = solved.astype(jnp.bfloat16)

    def apply(t, lag_here):
        field = fields[t]

        def row(b, carry):
            rows = pl.ds(pl.multiple_of(b * BLK, BLK), BLK)
            base = (lag_here * 8 + b) * 16
            left = jnp.concatenate([weights[lag_here, b, k] for k in range(16)], axis=1)
            right = jnp.concatenate(
                [field[column_ref[base + k]] for k in range(16)], axis=0
            )
            term = jnp.dot(left, right, preferred_element_type=jnp.float32)
            if lag_here < 2:
                above = waiting[lag_here + 1, rows, :]
            elif t == 0:
                above = behind0[rows, :]
            else:
                above = behind[t - 1, rows, :].astype(jnp.float32)
            waiting[lag_here, rows, :] = term + above
            return carry

        lax.fori_loop(0, 8, row, 0, unroll=8)

    def behind_copy(t, device):
        if t == 0:
            return pltpu.make_async_remote_copy(
                src_ref=pending_hbm.at[0], dst_ref=behind0, send_sem=send_sem.at[t, BEHIND],
                recv_sem=recv_sem.at[t, BEHIND], device_id=device, device_id_type=MESH,
            )
        return pltpu.make_async_remote_copy(
            src_ref=ahead.at[t - 1], dst_ref=behind.at[t - 1], send_sem=send_sem.at[t, BEHIND],
            recv_sem=recv_sem.at[t, BEHIND], device_id=device, device_id_type=MESH,
        )

    def pass_down(t):
        @pl.when(lag > 0)
        def _():
            if t > 0:
                ahead[t - 1] = waiting[0].astype(jnp.bfloat16)
            behind_copy(t, (lag - 1, patch)).start()

    def later_lags(t):
        apply(t, 1)

        @pl.when(lag < 7)
        def _():
            behind_copy(t, me).wait_recv()

        apply(t, 2)

    @pl.when(lag == 7)
    def _():
        behind0[...] = jnp.zeros_like(behind0)
        behind[...] = jnp.zeros_like(behind)

    pass_down(0)
    for copy_in in loads[:3]:
        copy_in.wait()

    for t in range(steps):

        @pl.when(lag == 0)
        def _():
            solve(t)
            first_sends(t)
            along_y(t)
            copy(t, piece(t, held()), at(z_lo=other_z, z_hi=1 - z_hi), OWN).start()

        if t == 0:
            loads[3].wait()
        else:
            later_lags(t - 1)

        @pl.when(lag > 0)
        def _():
            copy(t, piece(t, held()), me, OWN).wait_recv()

            @pl.when(lag == 4)
            def _():
                along_y(t)

            first_sends(t)

        relays(t)
        pltpu.make_async_copy(piece(t, patch), currents_hbm.at[t], store_sem.at[t]).start()
        apply(t, 0)
        if t + 1 < steps:
            pass_down(t + 1)

    later_lags(steps - 1)
    out = pltpu.make_async_copy(waiting, sums_hbm, store_sem.at[steps])
    out.start()

    for t in range(steps):
        own = piece(t, held())
        whole = [FROM_X, FROM_X + 1, FROM_X + 2, FROM_Z] + [SIB + i for i in range(5)]
        for index in whole:
            copy(t, own, me, index).wait_send()
        for i in range(3):
            for index in (DIAG_A + i, SIB + 5 + i):
                copy(t, piece(t, held(), 0, A_BLOCKS), me, index).wait_send()
            for index in (DIAG_B + i, SIB + 8 + i):
                copy(t, piece(t, held(), A_BLOCKS), me, index).wait_send()

        @pl.when(lag == 0)
        def _():
            copy(t, own, me, OWN).wait_send()

        @pl.when(y == 0)
        def _():
            for i in range(3):
                copy(t, own, me, OWN, LAG_SEND + i).wait_send()

        @pl.when(lag > 0)
        def _():
            behind_copy(t, me).wait_send()

        pltpu.make_async_copy(piece(t, patch), currents_hbm.at[t], store_sem.at[t]).wait()
    out.wait()


def per_device(excitation, pending, retarded_blocks, column_index, near_inverse, near_index):
    steps = excitation.shape[0]
    smem, hbm = pl.BlockSpec(memory_space=pltpu.SMEM), pl.BlockSpec(memory_space=pltpu.HBM)
    field = pltpu.VMEM((16 * BLOCKS, BLK, WIDTH), jnp.bfloat16)
    currents, sums = pl.pallas_call(
        functools.partial(kernel, steps),
        out_shape=(
            jax.ShapeDtypeStruct((steps, BLOCKS, BLK, WIDTH), jnp.bfloat16),
            jax.ShapeDtypeStruct(pending.shape, jnp.float32),
        ),
        in_specs=[smem, smem, hbm, hbm, hbm, hbm],
        out_specs=(hbm, hbm),
        scratch_shapes=[
            field, field, field, field,
            pltpu.VMEM(retarded_blocks.shape, jnp.bfloat16),
            pltpu.VMEM(excitation.shape, jnp.float32),
            pltpu.VMEM(near_inverse.shape, jnp.float32),
            pltpu.VMEM(pending.shape, jnp.float32),
            pltpu.VMEM((ROWS, WIDTH), jnp.float32),
            pltpu.VMEM((steps - 1, ROWS, WIDTH), jnp.bfloat16),
            pltpu.VMEM((steps - 1, ROWS, WIDTH), jnp.bfloat16),
            pltpu.SemaphoreType.DMA((4,)),
            pltpu.SemaphoreType.DMA((steps + 1,)),
            pltpu.SemaphoreType.DMA((steps, N_SEND)),
            pltpu.SemaphoreType.DMA((steps, N_RECV)),
        ],
        compiler_params=pltpu.CompilerParams(
            collective_id=0, has_side_effects=True, vmem_limit_bytes=58 * 2**20
        ),
    )(column_index.reshape(-1), near_index, excitation, pending, retarded_blocks, near_inverse)
    return currents.reshape(excitation.shape), sums


def solution(mesh):
    placed = (
        P(None, "patch", None),
        P("lag", "patch", None),
        P("lag", "patch", None, None, None),
        P("lag", "patch", None),
        P("patch", None, None),
        P("patch"),
    )
    return jax.shard_map(
        per_device,
        mesh=mesh,
        in_specs=placed,
        out_specs=(P(None, "patch", None), P("lag", "patch", None)),
        check_vma=False,
    )
```

time: 627 us -> 151 us (0.24)
  the two profiles are of different devices: /device:TPU:25 before, /device:TPU:95 now
where the time goes in v1:
time: 151 us
  Pallas kernels  145 us (96%)
  local copies, waits for them, and re-layouts  4.89 us (3%)
    pallas_call x1, Pallas kernels, per_device(): pl.pallas_call(functools.partial(kernel, steps), out_shape=(jax.ShapeDtyp...  145 us
    unnamed x4, local copies, waits for them, and re-layouts  3.53 us

profile of v1, /device:TPU:95, one launch (start us, length us, event | category | flops | bytes accessed | tf_op | source)
XLA Modules:
  0.0 150.5 jit_solution(9246239655183451)
XLA Ops:
  0.6 1.4 reshape.10.column_ref
  2.0 145.0 %shard_map.77 = (bf16[4,8,128,128]{3,2,1,0:T(8,128)(2,1)}, f32[3,1024,128]{2,1,0:T(8,128)}) custom-call(s32[384]{0:T(512)} %reshape.10.column_ref, s32[8]{0:T(128)} %near_ref.1, f32[4,1024,128]{2,1,0:T(8,128)} %excitation_hbm.1, f32[3,1024,128]{2,1,0:T(8,128)} %pending_hbm.1, bf16[3,8,16,128,128]{4,3,2,1,0:T(8,128)(2,1)} %weights_hbm.1, ...), custom_call_target="tpu_custom_call" | custom-call | tf_op jit(solution)/shard_map/pallas_call | solution.py:256
  147.0 0.0 copy-start
  147.0 2.4 %copy.10 = bf16[4,1024,128]{2,1,0:T(8,128)(2,1)} copy(bf16[4,1024,128]{2,1,0:T(8,128)(2,1)} %bitcast.1) | data formatting | bytes 2097152
  149.4 0.0 copy-done
  149.4 1.1 copy.11
Async XLA Ops:
  147.0 2.4 %copy-start = (f32[3,1024,128]{2,1,0:T(8,128)S(1)}, f32[3,1024,128]{2,1,0:T(8,128)}, u32[]{:S(2)}) copy-start(f32[3,1024,128]{2,1,0:T(8,128)} %get-tuple-element.9) | copy-start | bytes 4718596

commit v2 on v1

v2 whole, which is shorter than its diff:
```python
import functools

import jax
import jax.numpy as jnp
from jax import lax
from jax.experimental import pallas as pl
from jax.experimental.pallas import tpu as pltpu
from jax.sharding import PartitionSpec as P

MESH = pl.DeviceIdType.MESH
BLK = 128
WIDTH = 128
HALF = 64
BLOCKS = 8
PAIRS = 4
ROWS = BLOCKS * BLK
KB = 16
A_PAIRS = (2, 2)
SHIFTS = (1, 3, 2)

OWN, X_A, X_B, Z_A, Z_B, DIAG_A, DIAG_B, SIB, N_RECV = 0, 1, 4, 7, 8, 9, 12, 15, 23
LAG_SEND = 23
N_SEND = 26


def kernel(
    steps,
    pair_ref, side_ref, near_ref, excitation_hbm, pending_hbm, weights_hbm, inverse_hbm,
    currents_hbm, sums_hbm,
    f0, f1, f2, f3, f4, f5, f6, f7, weights, excitation, inverse, waiting, behind0, behind, ahead, currents, sides,
    load_sem, store_sem, down_send, down_recv, send_sem, recv_sem,
):
    fields = (f0, f1, f2, f3, f4, f5, f6, f7)
    units = 2 * steps
    lag, patch = lax.axis_index("lag"), lax.axis_index("patch")
    z_hi, y = lag // 4, lag % 4
    z_lo, x, core = patch // 8, (patch // 2) % 4, patch % 2

    def at(x=x, z_lo=z_lo, core=core, y=y, z_hi=z_hi):
        return (z_hi * 4 + y, z_lo * 8 + x * 2 + core)

    def held(x=x, z_lo=z_lo, core=core):
        return ((z_lo + z_hi) % 2) * 8 + x * 2 + core

    me = at()
    other_z, other_core = 1 - z_lo, 1 - core
    x_to = [(x + s) % 4 for s in SHIFTS]
    x_from = [(x + 4 - s) % 4 for s in SHIFTS]
    left_half = lax.broadcasted_iota(jnp.int32, (BLK, WIDTH), 1) < HALF

    loads = [
        pltpu.make_async_copy(pending_hbm, waiting, load_sem.at[0]),
        pltpu.make_async_copy(inverse_hbm, inverse, load_sem.at[1]),
        pltpu.make_async_copy(excitation_hbm, excitation, load_sem.at[2]),
        pltpu.make_async_copy(weights_hbm, weights, load_sem.at[3]),
    ]
    for load in loads:
        load.start()

    barrier = pltpu.get_barrier_semaphore()
    greeted = [at(x=to) for to in x_to] + [at(y=(y + s) % 4) for s in SHIFTS]
    greeted += [at(z_lo=other_z), at(core=other_core), at(z_lo=other_z, z_hi=1 - z_hi), at(y=3 - y, z_hi=1 - z_hi)]
    for device in greeted:
        pl.semaphore_signal(barrier, inc=1, device_id=device, device_id_type=MESH)
    pl.semaphore_wait(barrier, len(greeted))

    def piece(u, slab, low=0, high=PAIRS):
        return fields[u].at[pl.ds(slab * PAIRS + low, high - low)]

    def copy(u, ref, device, index, sender=None):
        return pltpu.make_async_remote_copy(
            src_ref=ref,
            dst_ref=ref,
            send_sem=send_sem.at[u, index if sender is None else sender],
            recv_sem=recv_sem.at[u, index],
            device_id=device,
            device_id_type=MESH,
        )

    def arrived(u, ref, index):
        copy(u, ref, me, index).wait_recv()

    def to_sibling(u, ref, index):
        copy(u, ref, at(core=other_core), SIB + index).start()

    def along_y(u):
        for i, s in enumerate(SHIFTS):
            copy(u, piece(u, held()), at(y=(y + s) % 4), OWN, LAG_SEND + i).start()

    def first_sends(u):
        cut = A_PAIRS[u % 2]
        own, first, second = piece(u, held()), piece(u, held(), 0, cut), piece(u, held(), cut)
        copy(u, second, at(z_lo=other_z), Z_B).start()
        for i, to in enumerate(x_to):
            copy(u, first, at(x=to), X_A + i).start()
        copy(u, first, at(z_lo=other_z), Z_A).start()
        to_sibling(u, own, 0)

    def relays(u):
        cut = A_PAIRS[u % 2]
        slab = held(z_lo=other_z)
        arrived(u, piece(u, slab, cut), Z_B)
        for i, to in enumerate(x_to):
            copy(u, piece(u, slab, cut), at(x=to), DIAG_B + i).start()
        for i, to in enumerate(x_to):
            copy(u, piece(u, held(), cut), at(x=to), X_B + i).start()

    def relays_z(u):
        cut = A_PAIRS[u % 2]
        for i in range(3):
            slab = held(x=x_from[i])
            arrived(u, piece(u, slab, 0, cut), X_A + i)
            copy(u, piece(u, slab, 0, cut), at(z_lo=other_z), DIAG_A + i).start()

    def share(u):
        cut = A_PAIRS[u % 2]
        slab = held(z_lo=other_z)
        arrived(u, piece(u, slab, 0, cut), Z_A)
        to_sibling(u, piece(u, slab), 4)
        for i in range(3):
            slab = held(x=x_from[i])
            arrived(u, piece(u, slab, cut), X_B + i)
            to_sibling(u, piece(u, slab), 1 + i)
        for i in range(3):
            slab = held(x=x_from[i], z_lo=other_z)
            arrived(u, piece(u, slab, cut), DIAG_B + i)
            arrived(u, piece(u, slab, 0, cut), DIAG_A + i)
            to_sibling(u, piece(u, slab), 5 + i)

    def complete(u):
        arrived(u, piece(u, held(core=other_core)), SIB)
        arrived(u, piece(u, held(z_lo=other_z, core=other_core)), SIB + 4)
        for i in range(3):
            arrived(u, piece(u, held(x=x_from[i], core=other_core)), SIB + 1 + i)
            arrived(u, piece(u, held(x=x_from[i], z_lo=other_z, core=other_core)), SIB + 5 + i)

    def swap(a):
        return pltpu.roll(a, HALF, 1)

    def solve(u):
        t, half = u // 2, u % 2
        for i in range(PAIRS):
            solved = []
            for b in (i, i + PAIRS):
                rows = pl.ds(b * BLK, BLK)
                rhs = excitation[t, rows, :] - waiting[0, rows, :]
                solved.append(
                    jnp.dot(inverse[near_ref[b]], rhs, precision=lax.Precision.HIGHEST, preferred_element_type=jnp.float32)
                )
            low, high = solved
            packed = jnp.where(left_half, low, swap(high)) if half == 0 else jnp.where(left_half, swap(low), high)
            fields[u][held() * PAIRS + i] = packed.astype(jnp.bfloat16)

    def apply(u, lag_here):
        t, half = u // 2, u % 2
        field = fields[u]
        mine = left_half if half == 0 else jnp.logical_not(left_half)

        def row(b, carry):
            rows = pl.ds(pl.multiple_of(b * BLK, BLK), BLK)
            base = (lag_here * BLOCKS + b) * KB
            left = jnp.concatenate([weights[lag_here, b, k] for k in range(KB)], axis=1)
            picked = []
            for k in range(KB):
                side = sides[side_ref[base + k]]
                picked.append(field[pair_ref[base + k]] * jnp.concatenate([side] * (BLK // 16), axis=0))
            term = jnp.dot(left, jnp.concatenate(picked, axis=0), preferred_element_type=jnp.float32)
            term = term + swap(term)
            if lag_here < 2:
                term = term + waiting[lag_here + 1, rows, :]
            waiting[lag_here, rows, :] = jnp.where(mine, term, waiting[lag_here, rows, :])
            return carry

        lax.fori_loop(0, BLOCKS, row, 0, unroll=4)

    def down_copy(t, device):
        if t == 0:
            return pltpu.make_async_remote_copy(
                src_ref=pending_hbm.at[0], dst_ref=behind0, send_sem=down_send.at[t],
                recv_sem=down_recv.at[t], device_id=device, device_id_type=MESH,
            )
        return pltpu.make_async_remote_copy(
            src_ref=ahead.at[t - 1], dst_ref=behind.at[t - 1], send_sem=down_send.at[t],
            recv_sem=down_recv.at[t], device_id=device, device_id_type=MESH,
        )

    def pass_down(t):
        @pl.when(lag > 0)
        def _():
            if t > 0:
                ahead[t - 1] = waiting[0].astype(jnp.bfloat16)
            down_copy(t, (lag - 1, patch)).start()

    def store(t):
        for i in range(PAIRS):
            first = fields[2 * t][patch * PAIRS + i].astype(jnp.float32)
            second = fields[2 * t + 1][patch * PAIRS + i].astype(jnp.float32)
            currents[t, i] = jnp.where(left_half, first, swap(second)).astype(jnp.bfloat16)
            currents[t, i + PAIRS] = jnp.where(left_half, swap(first), second).astype(jnp.bfloat16)
        pltpu.make_async_copy(currents.at[t], currents_hbm.at[t], store_sem.at[t]).start()

    pass_down(0)
    in_left = lax.broadcasted_iota(jnp.int32, (16, WIDTH), 1) < HALF
    sides[0] = jnp.where(in_left, 1.0, 0.0).astype(jnp.bfloat16)
    sides[1] = jnp.where(in_left, 0.0, 1.0).astype(jnp.bfloat16)

    for load in loads[:3]:
        load.wait()

    for u in range(units + 1):
        if u < units:

            @pl.when(lag == 0)
            def _():
                solve(u)
                copy(u, piece(u, held()), at(z_lo=other_z, z_hi=1 - z_hi), OWN).start()
                first_sends(u)
                along_y(u)

            @pl.when(lag > 0)
            def _():
                arrived(u, piece(u, held()), OWN)

                @pl.when(lag == 4)
                def _():
                    along_y(u)

                first_sends(u)

        if u == 1:
            loads[3].wait()

        if u >= 2:
            apply(u - 2, 1)
            apply(u - 2, 2)
        if u == 3:

            @pl.when(lag < 7)
            def _():
                down_copy(0, me).wait_recv()
                waiting[2] = waiting[2] + behind0[...]

        if u < units:
            relays(u)
        if u >= 1:
            share(u - 1)
        if u < units:
            relays_z(u)
        if u >= 3 and u % 2 == 1:
            store((u - 3) // 2)
        if u >= 1:
            complete(u - 1)
            apply(u - 1, 0)
        if u >= 2 and u % 2 == 0 and u // 2 < steps:
            pass_down(u // 2)

    apply(units - 1, 1)
    apply(units - 1, 2)

    @pl.when(lag < 7)
    def _():
        for t in range(1, steps):
            down_copy(t, me).wait_recv()
            waiting[t - 1] = waiting[t - 1] + behind[t - 1].astype(jnp.float32)

    out = pltpu.make_async_copy(waiting, sums_hbm, store_sem.at[steps])
    out.start()
    store(steps - 1)

    for u in range(units):
        cut = A_PAIRS[u % 2]
        own = piece(u, held())
        for i in range(8):
            copy(u, own, me, SIB + i).wait_send()
        for index in [X_A, X_A + 1, X_A + 2, Z_A, DIAG_A, DIAG_A + 1, DIAG_A + 2]:
            copy(u, piece(u, held(), 0, cut), me, index).wait_send()
        for index in [X_B, X_B + 1, X_B + 2, Z_B, DIAG_B, DIAG_B + 1, DIAG_B + 2]:
            copy(u, piece(u, held(), cut), me, index).wait_send()

        @pl.when(lag == 0)
        def _():
            copy(u, own, me, OWN).wait_send()

        @pl.when(y == 0)
        def _():
            for i in range(3):
                copy(u, own, me, OWN, LAG_SEND + i).wait_send()

    for t in range(steps):

        @pl.when(lag > 0)
        def _():
            down_copy(t, me).wait_send()

        pltpu.make_async_copy(currents.at[t], currents_hbm.at[t], store_sem.at[t]).wait()
    out.wait()


def per_device(excitation, pending, retarded_blocks, column_index, near_inverse, near_index):
    steps = excitation.shape[0]
    columns = column_index.reshape(-1)
    pairs = columns // BLOCKS * PAIRS + columns % PAIRS
    sides = columns // PAIRS % 2
    smem, hbm = pl.BlockSpec(memory_space=pltpu.SMEM), pl.BlockSpec(memory_space=pltpu.HBM)
    field = pltpu.VMEM((16 * PAIRS, BLK, WIDTH), jnp.bfloat16)
    currents, sums = pl.pallas_call(
        functools.partial(kernel, steps),
        out_shape=(
            jax.ShapeDtypeStruct((steps, BLOCKS, BLK, WIDTH), jnp.bfloat16),
            jax.ShapeDtypeStruct(pending.shape, jnp.float32),
        ),
        in_specs=[smem, smem, smem, hbm, hbm, hbm, hbm],
        out_specs=(hbm, hbm),
        scratch_shapes=[
            *[field] * 8,
            pltpu.VMEM(retarded_blocks.shape, jnp.bfloat16),
            pltpu.VMEM(excitation.shape, jnp.float32),
            pltpu.VMEM(near_inverse.shape, jnp.float32),
            pltpu.VMEM(pending.shape, jnp.float32),
            pltpu.VMEM((ROWS, WIDTH), jnp.float32),
            pltpu.VMEM((steps - 1, ROWS, WIDTH), jnp.bfloat16),
            pltpu.VMEM((steps - 1, ROWS, WIDTH), jnp.bfloat16),
            pltpu.VMEM((steps, BLOCKS, BLK, WIDTH), jnp.bfloat16),
            pltpu.VMEM((2, 16, WIDTH), jnp.bfloat16),
            pltpu.SemaphoreType.DMA((4,)),
            pltpu.SemaphoreType.DMA((steps + 1,)),
            pltpu.SemaphoreType.DMA((steps,)),
            pltpu.SemaphoreType.DMA((steps,)),
            pltpu.SemaphoreType.DMA((2 * steps, N_SEND)),
            pltpu.SemaphoreType.DMA((2 * steps, N_RECV)),
        ],
        compiler_params=pltpu.CompilerParams(
            collective_id=0, has_side_effects=True, vmem_limit_bytes=58 * 2**20
        ),
    )(pairs, sides, near_index, excitation, pending, retarded_blocks, near_inverse)
    return currents.reshape(excitation.shape), sums


def solution(mesh):
    placed = (
        P(None, "patch", None),
        P("lag", "patch", None),
        P("lag", "patch", None, None, None),
        P("lag", "patch", None),
        P("patch", None, None),
        P("patch"),
    )
    return jax.shard_map(
        per_device,
        mesh=mesh,
        in_specs=placed,
        out_specs=(P(None, "patch", None), P("lag", "patch", None)),
        check_vma=False,
    )
```

time: 151 us -> 123 us (0.81)
  the two profiles are of different devices: /device:TPU:95 before, /device:TPU:89 now
where the time goes in v2:
time: 123 us
  Pallas kernels  117 us (95%)
  local copies, waits for them, and re-layouts  4.31 us (4%)
    pallas_call x1, Pallas kernels, per_device(): pl.pallas_call(functools.partial(kernel, steps), out_shape=(jax.ShapeDtyp...  117 us
    unnamed x4, local copies, waits for them, and re-layouts  3.53 us

profile of v2, /device:TPU:89, one launch (start us, length us, event | category | flops | bytes accessed | tf_op | source)
XLA Modules:
  0.0 122.5 jit_solution(15397557953593872084)
XLA Ops:
  0.6 0.8 reshape.10
  1.4 0.6 add_select_fusion
  2.0 117.0 %shard_map.77 = (bf16[4,8,128,128]{3,2,1,0:T(8,128)(2,1)}, f32[3,1024,128]{2,1,0:T(8,128)}) custom-call(s32[384]{0:T(512)} %get-tuple-element.7.pair_ref, s32[384]{0:T(512)} %get-tuple-element.6.side_ref, s32[8]{0:T(128)} %near_ref.1, f32[4,1024,128]{2,1,0:T(8,128)} %excitation_hbm.1, f32[3,1024,128]{2,1,0:T(8,128)} %pending_hbm.1, ...), custom_call_target="tpu_custom_call" | custom-call | tf_op jit(solution)/shard_map/pallas_call | solution.py:306
  119.0 0.0 copy-start
  119.0 2.4 %copy.10 = bf16[4,1024,128]{2,1,0:T(8,128)(2,1)} copy(bf16[4,1024,128]{2,1,0:T(8,128)(2,1)} %bitcast.1) | data formatting | bytes 2097152
  121.4 0.0 copy-done
  121.4 1.1 copy.11
Async XLA Ops:
  119.0 2.4 %copy-start = (f32[3,1024,128]{2,1,0:T(8,128)S(1)}, f32[3,1024,128]{2,1,0:T(8,128)}, u32[]{:S(2)}) copy-start(f32[3,1024,128]{2,1,0:T(8,128)} %get-tuple-element.11) | copy-start | bytes 4718596

commit v3 on v2

--- a/solution.py
+++ b/solution.py
@@ -27,8 +27,8 @@
     steps,
     pair_ref, side_ref, near_ref, excitation_hbm, pending_hbm, weights_hbm, inverse_hbm,
     currents_hbm, sums_hbm,
-    f0, f1, f2, f3, f4, f5, f6, f7, weights, excitation, inverse, waiting, behind0, behind, ahead, currents, sides,
-    load_sem, store_sem, down_send, down_recv, send_sem, recv_sem,
+    f0, f1, f2, f3, f4, f5, f6, f7, weights, excitation, inverse, waiting, behind0, behind, ahead, crossing, currents, sides,
+    load_sem, store_sem, down_send, down_recv, cross_send, cross_recv, send_sem, recv_sem,
 ):
     fields = (f0, f1, f2, f3, f4, f5, f6, f7)
     units = 2 * steps
@@ -60,6 +60,7 @@
     barrier = pltpu.get_barrier_semaphore()
     greeted = [at(x=to) for to in x_to] + [at(y=(y + s) % 4) for s in SHIFTS]
     greeted += [at(z_lo=other_z), at(core=other_core), at(z_lo=other_z, z_hi=1 - z_hi), at(y=3 - y, z_hi=1 - z_hi)]
+    greeted += [at(y=3 - y, z_hi=1 - z_hi, z_lo=other_z)]
     for device in greeted:
         pl.semaphore_signal(barrier, inc=1, device_id=device, device_id_type=MESH)
     pl.semaphore_wait(barrier, len(greeted))
@@ -189,7 +190,34 @@
         def _():
             if t > 0:
                 ahead[t - 1] = waiting[0].astype(jnp.bfloat16)
-            down_copy(t, (lag - 1, patch)).start()
+
+            @pl.when(jnp.logical_or(t == 0, lag != 4))
+            def _():
+                down_copy(t, (lag - 1, patch)).start()
+
+            if t > 0:
+
+                @pl.when(lag == 4)
+                def _():
+                    cross_copy(t, at(y=3, z_hi=0, z_lo=other_z)).start()
+
+    def cross_copy(t, device):
+        return pltpu.make_async_remote_copy(
+            src_ref=ahead.at[t - 1], dst_ref=crossing.at[t - 1], send_sem=cross_send.at[t - 1],
+            recv_sem=cross_recv.at[t - 1], device_id=device, device_id_type=MESH,
+        )
+
+    def crossed_copy(t, device):
+        return pltpu.make_async_remote_copy(
+            src_ref=crossing.at[t - 1], dst_ref=behind.at[t - 1], send_sem=cross_send.at[t - 1],
+            recv_sem=down_recv.at[t], device_id=device, device_id_type=MESH,
+        )
+
+    def cross(t):
+        @pl.when(lag == 3)
+        def _():
+            cross_copy(t, me).wait_recv()
+            crossed_copy(t, at(z_lo=other_z)).start()
 
     def store(t):
         for i in range(PAIRS):
@@ -247,6 +275,8 @@
         if u < units:
             relays_z(u)
         if u >= 3 and u % 2 == 1:
+            cross(u // 2)
+        if u >= 3 and u % 2 == 1:
             store((u - 3) // 2)
         if u >= 1:
             complete(u - 1)
@@ -288,9 +318,15 @@
 
     for t in range(steps):
 
-        @pl.when(lag > 0)
+        @pl.when(jnp.logical_and(lag > 0, jnp.logical_or(t == 0, lag != 4)))
         def _():
             down_copy(t, me).wait_send()
+
+        if t > 0:
+
+            @pl.when(jnp.logical_or(lag == 3, lag == 4))
+            def _():
+                cross_copy(t, me).wait_send()
 
         pltpu.make_async_copy(currents.at[t], currents_hbm.at[t], store_sem.at[t]).wait()
     out.wait()
@@ -320,12 +356,15 @@
             pltpu.VMEM((ROWS, WIDTH), jnp.float32),
             pltpu.VMEM((steps - 1, ROWS, WIDTH), jnp.bfloat16),
             pltpu.VMEM((steps - 1, ROWS, WIDTH), jnp.bfloat16),
+            pltpu.VMEM((steps - 1, ROWS, WIDTH), jnp.bfloat16),
             pltpu.VMEM((steps, BLOCKS, BLK, WIDTH), jnp.bfloat16),
             pltpu.VMEM((2, 16, WIDTH), jnp.bfloat16),
             pltpu.SemaphoreType.DMA((4,)),
             pltpu.SemaphoreType.DMA((steps + 1,)),
             pltpu.SemaphoreType.DMA((steps,)),
             pltpu.SemaphoreType.DMA((steps,)),
+            pltpu.SemaphoreType.DMA((steps - 1,)),
+            pltpu.SemaphoreType.DMA((steps - 1,)),
             pltpu.SemaphoreType.DMA((2 * steps, N_SEND)),
             pltpu.SemaphoreType.DMA((2 * steps, N_RECV)),
         ],

time: 123 us -> 113 us (0.919)
  the two profiles are of different devices: /device:TPU:89 before, /device:TPU:25 now
where the time goes in v3:
time: 113 us; the launch traced here: 112 us
  Pallas kernels  107 us (95%)
  local copies, waits for them, and re-layouts  4.31 us (4%)
    pallas_call x1, Pallas kernels, per_device(): pl.pallas_call(functools.partial(kernel, steps), out_shape=(jax.ShapeDtyp...  107 us
    unnamed x4, local copies, waits for them, and re-layouts  3.53 us

profile of v3, /device:TPU:25, one launch (start us, length us, event | category | flops | bytes accessed | tf_op | source)
XLA Modules:
  0.0 112.4 jit_solution(9360404954651092723)
XLA Ops:
  0.6 0.8 reshape.10
  1.4 0.6 add_select_fusion
  2.0 106.8 %shard_map.77 = (bf16[4,8,128,128]{3,2,1,0:T(8,128)(2,1)}, f32[3,1024,128]{2,1,0:T(8,128)}) custom-call(s32[384]{0:T(512)} %get-tuple-element.7.pair_ref, s32[384]{0:T(512)} %get-tuple-element.6.side_ref, s32[8]{0:T(128)} %near_ref.1, f32[4,1024,128]{2,1,0:T(8,128)} %excitation_hbm.1, f32[3,1024,128]{2,1,0:T(8,128)} %pending_hbm.1, ...), custom_call_target="tpu_custom_call" | custom-call | tf_op jit(solution)/shard_map/pallas_call | solution.py:342
  108.9 0.0 copy-start
  108.9 2.4 %copy.10 = bf16[4,1024,128]{2,1,0:T(8,128)(2,1)} copy(bf16[4,1024,128]{2,1,0:T(8,128)(2,1)} %bitcast.1) | data formatting | bytes 2097152
  111.3 0.0 copy-done
  111.3 1.1 %copy.11 = f32[3,1024,128]{2,1,0:T(8,128)} copy(f32[3,1024,128]{2,1,0:T(8,128)S(1)} %copy-done) | data formatting | bytes 3145728
Async XLA Ops:
  108.9 2.4 %copy-start = (f32[3,1024,128]{2,1,0:T(8,128)S(1)}, f32[3,1024,128]{2,1,0:T(8,128)}, u32[]{:S(2)}) copy-start(f32[3,1024,128]{2,1,0:T(8,128)} %get-tuple-element.11) | copy-start | bytes 4718596

commit v4 on v3

--- a/solution.py
+++ b/solution.py
@@ -91,9 +91,9 @@
     def first_sends(u):
         cut = A_PAIRS[u % 2]
         own, first, second = piece(u, held()), piece(u, held(), 0, cut), piece(u, held(), cut)
-        copy(u, second, at(z_lo=other_z), Z_B).start()
         for i, to in enumerate(x_to):
             copy(u, first, at(x=to), X_A + i).start()
+        copy(u, second, at(z_lo=other_z), Z_B).start()
         copy(u, first, at(z_lo=other_z), Z_A).start()
         to_sibling(u, own, 0)
 
@@ -284,6 +284,7 @@
         if u >= 2 and u % 2 == 0 and u // 2 < steps:
             pass_down(u // 2)
 
+    store(steps - 1)
     apply(units - 1, 1)
     apply(units - 1, 2)
 
@@ -295,7 +296,6 @@
 
     out = pltpu.make_async_copy(waiting, sums_hbm, store_sem.at[steps])
     out.start()
-    store(steps - 1)
 
     for u in range(units):
         cut = A_PAIRS[u % 2]

time: 113 us -> 113 us (level)
  no operation moved by 1% of the time
where the time goes in v4:
time: 113 us
  Pallas kernels  107 us (95%)
  local copies, waits for them, and re-layouts  4.31 us (4%)
    pallas_call x1, Pallas kernels, per_device(): pl.pallas_call(functools.partial(kernel, steps), out_shape=(jax.ShapeDtyp...  107 us
    unnamed x4, local copies, waits for them, and re-layouts  3.53 us

profile of v4, /device:TPU:25, one launch (start us, length us, event | category | flops | bytes accessed | tf_op | source)
XLA Modules:
  0.0 112.6 jit_solution(16475970494306003046)
XLA Ops:
  0.6 0.8 reshape.10
  1.4 0.6 add_select_fusion
  2.0 107.1 %shard_map.77 = (bf16[4,8,128,128]{3,2,1,0:T(8,128)(2,1)}, f32[3,1024,128]{2,1,0:T(8,128)}) custom-call(s32[384]{0:T(512)} %get-tuple-element.7.pair_ref, s32[384]{0:T(512)} %get-tuple-element.6.side_ref, s32[8]{0:T(128)} %near_ref.1, f32[4,1024,128]{2,1,0:T(8,128)} %excitation_hbm.1, f32[3,1024,128]{2,1,0:T(8,128)} %pending_hbm.1, ...), custom_call_target="tpu_custom_call" | custom-call | tf_op jit(solution)/shard_map/pallas_call | solution.py:342
  109.1 0.0 copy-start
  109.1 2.4 %copy.10 = bf16[4,1024,128]{2,1,0:T(8,128)(2,1)} copy(bf16[4,1024,128]{2,1,0:T(8,128)(2,1)} %bitcast.1) | data formatting | bytes 2097152
  111.5 0.0 copy-done
  111.5 1.1 %copy.11 = f32[3,1024,128]{2,1,0:T(8,128)} copy(f32[3,1024,128]{2,1,0:T(8,128)S(1)} %copy-done) | data formatting | bytes 3145728
Async XLA Ops:
  109.1 2.4 %copy-start = (f32[3,1024,128]{2,1,0:T(8,128)S(1)}, f32[3,1024,128]{2,1,0:T(8,128)}, u32[]{:S(2)}) copy-start(f32[3,1024,128]{2,1,0:T(8,128)} %get-tuple-element.11) | copy-start | bytes 4718596

commit v5 on v3

--- a/solution.py
+++ b/solution.py
@@ -172,7 +172,8 @@
             waiting[lag_here, rows, :] = jnp.where(mine, term, waiting[lag_here, rows, :])
             return carry
 
-        lax.fori_loop(0, BLOCKS, row, 0, unroll=4)
+        unroll = 8 if lag_here == 0 else 4 if u == units - 1 else 2
+        lax.fori_loop(0, BLOCKS, row, 0, unroll=unroll)
 
     def down_copy(t, device):
         if t == 0:

time: 113 us -> 114 us (level)
  no operation moved by 1% of the time
where the time goes in v5:
time: 114 us; the launch traced here: 113 us
  Pallas kernels  108 us (95%)
  local copies, waits for them, and re-layouts  4.31 us (4%)
    pallas_call x1, Pallas kernels, per_device(): pl.pallas_call(functools.partial(kernel, steps), out_shape=(jax.ShapeDtyp...  108 us
    unnamed x4, local copies, waits for them, and re-layouts  3.53 us

profile of v5, /device:TPU:25, one launch (start us, length us, event | category | flops | bytes accessed | tf_op | source)
XLA Modules:
  0.0 113.4 jit_solution(13211177074579677627)
XLA Ops:
  0.6 0.8 reshape.10
  1.4 0.6 add_select_fusion
  2.0 107.8 %shard_map.77 = (bf16[4,8,128,128]{3,2,1,0:T(8,128)(2,1)}, f32[3,1024,128]{2,1,0:T(8,128)}) custom-call(s32[384]{0:T(512)} %get-tuple-element.7.pair_ref, s32[384]{0:T(512)} %get-tuple-element.6.side_ref, s32[8]{0:T(128)} %near_ref.1, f32[4,1024,128]{2,1,0:T(8,128)} %excitation_hbm.1, f32[3,1024,128]{2,1,0:T(8,128)} %pending_hbm.1, ...), custom_call_target="tpu_custom_call" | custom-call | tf_op jit(solution)/shard_map/pallas_call | solution.py:343
  109.8 0.0 copy-start
  109.8 2.4 %copy.10 = bf16[4,1024,128]{2,1,0:T(8,128)(2,1)} copy(bf16[4,1024,128]{2,1,0:T(8,128)(2,1)} %bitcast.1) | data formatting | bytes 2097152
  112.2 0.0 copy-done
  112.2 1.1 %copy.11 = f32[3,1024,128]{2,1,0:T(8,128)} copy(f32[3,1024,128]{2,1,0:T(8,128)S(1)} %copy-done) | data formatting | bytes 3145728
Async XLA Ops:
  109.8 2.4 %copy-start = (f32[3,1024,128]{2,1,0:T(8,128)S(1)}, f32[3,1024,128]{2,1,0:T(8,128)}, u32[]{:S(2)}) copy-start(f32[3,1024,128]{2,1,0:T(8,128)} %get-tuple-element.11) | copy-start | bytes 4718596
